TPU v7x, 32 devices: a whole 2x2x4 slice. The times are simulated.
32 devices in a mesh: slot: 8 (over y, x, core), own: 4 (over z).
Axes of the slice: x: 2, y: 2, z: 4, core: 2. Of those that a mesh axis runs over, the one named last changes fastest.
Arguments:
- slot_grads: bfloat16 [32, 768, 2048], P(('slot', 'own')), may hold values from -6 to 6
- weights: bfloat16 [16, 768, 2048], P(None, 'slot', 'own'), may hold values from -0.21875 to 0.21875
- moment: float32 [16, 768, 2048], P(None, 'slot', 'own'), may hold values from -2 to 2
- second: float32 [16, 768, 2048], P(None, 'slot', 'own'), may hold values from 0.01 to 1
- counts_old: int32 [16], replicated, may hold values from 1 to 4, as said below
- counts_new: int32 [16], replicated, may hold values from 1 to 4, as said below
- inputs: bfloat16 [8192, 768], P(('slot', 'own')), may hold values from -6 to 6
- row_slot: int32 [8192, 1], P(('slot', 'own')), may hold values from 0 to 31; in each aligned block of 256 rows (0 to 255, 256 to 511, ...) at most 16 rows name the same one
Outputs:
- new_weights: bfloat16 [16, 768, 2048], P(None, 'slot', 'own')
- new_moment: float32 [16, 768, 2048], P(None, 'slot', 'own')
- new_second: float32 [16, 768, 2048], P(None, 'slot', 'own')
- outputs: bfloat16 [8192, 2048], P(('slot', 'own'))
Inputs may be any that keep to these rules, and one draw needn't show every extreme that they name: counts_old sums to 32; some expert has 4 replicas and some has 1. counts_new sums to 32; some expert has 4 replicas and some has 1. `row_slot`: the 256 rows of one device name any one slot at most 16 times, a bound that some block reaches.
All inputs are finite; a program needn't handle non-finite values.
Results may differ from a plain program's by a relative error of at most 0.0049.
Values may be sent and summed in bfloat16 or wider, within the bound.
A program may use at most 128 MiB of HBM per device.

v0:
```python
import jax
import jax.numpy as jnp
from jax import lax
from jax.sharding import PartitionSpec as P


def slot_table(counts, n_slots):
    bounds = jnp.cumsum(counts)
    slots = jnp.arange(n_slots, dtype=jnp.int32)
    return jnp.sum((bounds[None, :] <= slots[:, None]).astype(jnp.int32), axis=1)


def body(slot_grads, weights, moment, second, counts_old, counts_new, inputs, row_slot):
    n_slot = lax.axis_size("slot")
    n_own = lax.axis_size("own")
    devices = n_slot * n_own
    experts, rows_here, cols_here = weights.shape
    width = slot_grads.shape[2]
    hidden = slot_grads.shape[1]
    tok_rows = inputs.shape[0]
    capacity = 2 * tok_rows // devices
    table_old = slot_table(counts_old, devices)
    table_new = slot_table(counts_new, devices)
    target = row_slot[:, 0]
    marks = (target[:, None] == jnp.arange(devices, dtype=jnp.int32)[None, :]).astype(jnp.int32)
    before = jnp.cumsum(marks, axis=0) - marks
    rank = jnp.sum(before * marks, axis=1)
    position = target * capacity + rank
    outgoing = jnp.zeros((devices * capacity, hidden), jnp.bfloat16).at[position].set(inputs)
    arrived = lax.all_to_all(
        outgoing.reshape(devices, capacity, hidden),
        ("slot", "own"),
        split_axis=0,
        concat_axis=0,
        tiled=True,
    )
    arrived = arrived.reshape(devices * capacity, hidden)
    sectioned = (
        slot_grads.reshape(n_slot, rows_here, n_own, cols_here)
        .transpose(0, 2, 1, 3)
        .reshape(devices, rows_here, cols_here)
    )
    pieces = lax.all_to_all(sectioned, ("slot", "own"), split_axis=0, concat_axis=0, tiled=True)
    source = jnp.arange(devices, dtype=jnp.int32)
    owner_of = table_old[source]
    select = (owner_of[None, :] == jnp.arange(experts, dtype=jnp.int32)[:, None]).astype(
        jnp.bfloat16
    )
    grads = jnp.dot(
        select, pieces.reshape(devices, rows_here * cols_here), preferred_element_type=jnp.float32
    ).reshape(experts, rows_here, cols_here)
    new_moment = 0.9 * moment + 0.1 * grads
    new_second = 0.95 * second + 0.05 * grads * grads
    bias_one = 1.0 - 0.9**10
    bias_two = 1.0 - 0.95**10
    update = 0.001 * (new_moment / bias_one) / (jnp.sqrt(new_second / bias_two) + 1e-08)
    new_weights = (weights.astype(jnp.float32) - update).astype(jnp.bfloat16)
    hosted = new_weights[table_new]
    landed = lax.all_to_all(hosted, ("slot", "own"), split_axis=0, concat_axis=0, tiled=True)
    slot_weight = (
        landed.reshape(n_slot, n_own, rows_here, cols_here)
        .transpose(0, 2, 1, 3)
        .reshape(hidden, width)
    )
    produced = jnp.dot(arrived, slot_weight, preferred_element_type=jnp.float32).astype(
        jnp.bfloat16
    )
    returned = lax.all_to_all(
        produced.reshape(devices, capacity, width),
        ("slot", "own"),
        split_axis=0,
        concat_axis=0,
        tiled=True,
    )
    outputs = returned.reshape(devices * capacity, width)[position]
    return (new_weights, new_moment, new_second, outputs)


def solution(mesh):
    placed = (
        P(("slot", "own"), None, None),
        P(None, "slot", "own"),
        P(None, "slot", "own"),
        P(None, "slot", "own"),
        P(),
        P(),
        P(("slot", "own"), None),
        P(("slot", "own"), None),
    )
    return jax.shard_map(
        body,
        mesh=mesh,
        in_specs=placed,
        out_specs=(
            P(None, "slot", "own"),
            P(None, "slot", "own"),
            P(None, "slot", "own"),
            P(("slot", "own"), None),
        ),
        check_vma=False,
    )
```

profile of v0, /device:TPU:0, one launch (start us, length us, event | category | flops | bytes accessed | tf_op | source)
XLA Modules:
  0.0 258.5 jit_solution(17244870331554456816)
XLA Ops:
  0.6 4.8 %reshape.118 = bf16[8,96,4,512]{3,2,1,0:T(4,128)(2,1)S(1)} reshape(bf16[1,768,2048]{2,1,0:T(8,128)(2,1)} %param.8) | data formatting | bytes 6291456 | tf_op jit(solution)/shard_map/reshape | solution.py:39
  5.4 2.5 copy.48
  7.9 0.0 copy-start.3
  7.9 0.0 copy-start.4
  7.9 7.3 %all-to-all-start = ((bf16[32,96,512]{2,1,0:T(8,128)(2,1)}), bf16[32,96,512]{2,1,0:T(8,128)(2,1)S(1)}, u32[]{:S(2)}, u32[]{:S(2)}) async-start(bf16[32,96,512]{2,1,0:T(8,128)(2,1)} %bitcast.3), calls=%async_computation | async-start | bytes 6291456 | tf_op jit(solution)/shard_map/all_to_all | solution.py:43
  15.2 0.0 copy-done.3
  15.2 0.1 copy.47
  15.3 0.1 reduce
  15.5 0.0 copy-done.4
  15.5 0.1 copy.52
  15.6 0.1 reduce.2
  15.7 0.1 convert_reduce_fusion.1
  15.8 0.7 gather_fusion
  16.5 0.1 convert_reduce_fusion
  16.6 68.8 %all-to-all-done = bf16[32,96,512]{2,1,0:T(8,128)(2,1)S(1)} async-done(((bf16[32,96,512]{2,1,0:T(8,128)(2,1)}), bf16[32,96,512]{2,1,0:T(8,128)(2,1)S(1)}, u32[]{:S(2)}, u32[]{:S(2)}) %all-to-all-start) | async-done | bytes 3145760 | tf_op jit(solution)/shard_map/all_to_all | solution.py:43
  85.4 11.6 %subtract_convert_fusion = (bf16[16,96,512]{2,0,1:T(8,128)(2,1)S(1)}, f32[16,96,512]{2,0,1:T(8,128)}, f32[16,96,512]{2,0,1:T(8,128)}) fusion(bf16[16,96,512]{2,1,0:T(8,128)(2,1)} %param.9, f32[16,96,512]{2,1,0:T(8,128)} %param.10, f32[16,96,512]{2,1,0:T(8,128)} %param.11, s32[32]{0:T(128)S(1)} %gather_fusion, bf16[4,8,96,512]{3,2,1,0:T(8,128)(2,1)S(1)} %bitcast.64), kind=kOutput, calls=%fused_computation.12 | convolution fusion | flops 61342208 | bytes 18874496 | tf_op jit(solution)/shard_map/dot_general | solution.py:49
  97.0 0.9 copy.55
  97.9 0.0 copy-start
  97.9 2.4 gather_fusion.1
  100.3 0.0 copy-done
  100.3 0.0 copy-start.2
  100.3 4.9 %all-to-all-start.2 = ((bf16[32,96,512]{2,1,0:T(8,128)(2,1)}), bf16[32,96,512]{2,1,0:T(8,128)(2,1)S(1)}, u32[]{:S(2)}, u32[]{:S(2)}) async-start(bf16[32,96,512]{2,1,0:T(8,128)(2,1)} %gather_fusion.1), calls=%async_computation.2 | async-start | bytes 6291456 | tf_op jit(solution)/shard_map/all_to_all | solution.py:59
  105.2 0.0 copy-done.2
  105.2 0.6 reduce-window.27
  105.8 0.2 slice_reduce_fusion
  106.0 0.1 fusion.9
  106.1 3.0 %scatter_custom_fusion = bf16[512,768]{1,0:T(8,128)(2,1)} fusion(s32[256]{0:T(256)S(1)} %bitcast.70, bf16[256,768]{1,0:T(8,128)(2,1)} %param.14, bf16[]{:T(256)} %constant.36.clone.1), kind=kCustom, calls=%fused_computation.14 | custom fusion | bytes 786944 | tf_op jit(solution)/shard_map/scatter | solution.py:29
  109.2 66.2 %all-to-all-done.2 = bf16[32,96,512]{2,1,0:T(8,128)(2,1)S(1)} async-done(((bf16[32,96,512]{2,1,0:T(8,128)(2,1)}), bf16[32,96,512]{2,1,0:T(8,128)(2,1)S(1)}, u32[]{:S(2)}, u32[]{:S(2)}) %all-to-all-start.2) | async-done | bytes 3145760 | tf_op jit(solution)/shard_map/all_to_all | solution.py:59
  175.3 5.2 %all-to-all-start.1 = ((bf16[32,16,768]{2,1,0:T(8,128)(2,1)}), bf16[32,16,768]{2,1,0:T(8,128)(2,1)}, u32[]{:S(2)}, u32[]{:S(2)}) async-start(bf16[32,16,768]{2,1,0:T(8,128)(2,1)} %bitcast.66), calls=%async_computation.1 | async-start | bytes 1572864 | tf_op jit(solution)/shard_map/all_to_all | solution.py:30
  180.5 2.4 copy.54
  182.9 1.0 copy.61
  184.0 16.0 %all-to-all-done.1 = bf16[32,16,768]{2,1,0:T(8,128)(2,1)} async-done(((bf16[32,16,768]{2,1,0:T(8,128)(2,1)}), bf16[32,16,768]{2,1,0:T(8,128)(2,1)}, u32[]{:S(2)}, u32[]{:S(2)}) %all-to-all-start.1) | async-done | bytes 786464 | tf_op jit(solution)/shard_map/all_to_all | solution.py:30
  199.9 4.3 %convolution_convert_fusion = bf16[512,2048]{1,0:T(8,128)(2,1)} fusion(bf16[512,768]{1,0:T(8,128)(2,1)} %bitcast.11, bf16[768,2048]{1,0:T(8,128)(2,1)S(1)} %bitcast.65), kind=kOutput, calls=%fused_computation.13 | convolution fusion | flops 1611661312 | bytes 6029312 | tf_op jit(solution)/shard_map/dot_general | solution.py:65
  204.2 4.4 %all-to-all-start.3 = ((bf16[32,16,2048]{2,1,0:T(8,128)(2,1)}), bf16[32,16,2048]{2,1,0:T(8,128)(2,1)S(1)}, u32[]{:S(2)}, u32[]{:S(2)}) async-start(bf16[32,16,2048]{2,1,0:T(8,128)(2,1)} %bitcast.67), calls=%async_computation.3 | async-start | bytes 4194304 | tf_op jit(solution)/shard_map/all_to_all | solution.py:68
  208.6 0.0 copy-start.1
  208.6 5.5 %copy.56 = f32[16,96,512]{2,1,0:T(8,128)} copy(f32[16,96,512]{2,0,1:T(8,128)} %get-tuple-element.21) | data formatting | bytes 6291456
  214.2 0.0 copy-done.1
  214.2 3.5 %copy.57 = f32[16,96,512]{2,1,0:T(8,128)} copy(f32[16,96,512]{2,0,1:T(8,128)S(1)} %copy-done.1) | data formatting | bytes 6291456
  217.6 38.5 %all-to-all-done.3 = bf16[32,16,2048]{2,1,0:T(8,128)(2,1)S(1)} async-done(((bf16[32,16,2048]{2,1,0:T(8,128)(2,1)}), bf16[32,16,2048]{2,1,0:T(8,128)(2,1)S(1)}, u32[]{:S(2)}, u32[]{:S(2)}) %all-to-all-start.3) | async-done | bytes 2097184 | tf_op jit(solution)/shard_map/all_to_all | solution.py:68
  256.1 2.3 gather_fusion.2
  (11 shorter events, 0.2 us)
Async XLA Ops:
  7.9 7.3 %copy-start.3 = (s32[16]{0:T(128)S(1)}, s32[16]{0:T(128)}, u32[]{:S(2)}) copy-start(s32[16]{0:T(128)} %param.12) | copy-start | bytes 196
  7.9 7.6 %copy-start.4 = (s32[16]{0:T(128)S(1)}, s32[16]{0:T(128)}, u32[]{:S(2)}) copy-start(s32[16]{0:T(128)} %param.13) | copy-start | bytes 196
  7.9 77.5 %all-to-all-start = ((bf16[32,96,512]{2,1,0:T(8,128)(2,1)}), bf16[32,96,512]{2,1,0:T(8,128)(2,1)S(1)}, u32[]{:S(2)}, u32[]{:S(2)}) async-start(bf16[32,96,512]{2,1,0:T(8,128)(2,1)} %bitcast.3), calls=%async_computation | async-start | bytes 6291456 | tf_op jit(solution)/shard_map/all_to_all | solution.py:43
  97.9 2.4 copy-start
  100.3 4.9 %copy-start.2 = (s32[256,1]{0,1:T(1,128)S(1)}, s32[256,1]{0,1:T(1,128)}, u32[]{:S(2)}) copy-start(s32[256,1]{0,1:T(1,128)} %param.15) | copy-start | bytes 3076
  100.3 75.0 %all-to-all-start.2 = ((bf16[32,96,512]{2,1,0:T(8,128)(2,1)}), bf16[32,96,512]{2,1,0:T(8,128)(2,1)S(1)}, u32[]{:S(2)}, u32[]{:S(2)}) async-start(bf16[32,96,512]{2,1,0:T(8,128)(2,1)} %gather_fusion.1), calls=%async_computation.2 | async-start | bytes 6291456 | tf_op jit(solution)/shard_map/all_to_all | solution.py:59
  175.3 24.6 %all-to-all-start.1 = ((bf16[32,16,768]{2,1,0:T(8,128)(2,1)}), bf16[32,16,768]{2,1,0:T(8,128)(2,1)}, u32[]{:S(2)}, u32[]{:S(2)}) async-start(bf16[32,16,768]{2,1,0:T(8,128)(2,1)} %bitcast.66), calls=%async_computation.1 | async-start | bytes 1572864 | tf_op jit(solution)/shard_map/all_to_all | solution.py:30
  204.2 51.9 %all-to-all-start.3 = ((bf16[32,16,2048]{2,1,0:T(8,128)(2,1)}), bf16[32,16,2048]{2,1,0:T(8,128)(2,1)S(1)}, u32[]{:S(2)}, u32[]{:S(2)}) async-start(bf16[32,16,2048]{2,1,0:T(8,128)(2,1)} %bitcast.67), calls=%async_computation.3 | async-start | bytes 4194304 | tf_op jit(solution)/shard_map/all_to_all | solution.py:68
  208.6 5.5 %copy-start.1 = (f32[16,96,512]{2,0,1:T(8,128)S(1)}, f32[16,96,512]{2,0,1:T(8,128)}, u32[]{:S(2)}) copy-start(f32[16,96,512]{2,0,1:T(8,128)} %get-tuple-element.22) | copy-start | bytes 9437188
where the time goes:
time: 260 us; the launch traced here: 258 us
  waiting for transfers between devices  189 us (73%)
  local copies, waits for them, and re-layouts  29.4 us (11%)
  starting transfers between devices  21.7 us (8%)
  matrix products  15.9 us (6%)
    all_to_all x1, waiting for transfers between devices, body(): lax.all_to_all(sectioned, ('slot', 'own'), split_axis=0, concat_axis=0, t...  68.8 us
    all_to_all x1, waiting for transfers between devices, body(): lax.all_to_all(hosted, ('slot', 'own'), split_axis=0, concat_axis=0, tile...  66.2 us
    all_to_all x1, waiting for transfers between devices, body(): lax.all_to_all(produced.reshape(devices, capacity, width), ('slot', 'own'...  38.5 us
    all_to_all x1, waiting for transfers between devices, body(): lax.all_to_all(outgoing.reshape(devices, capacity, hidden), ('slot', 'own...  16 us
    dot_general x1, matrix products, body(): jnp.dot(select, pieces.reshape(devices, rows_here * cols_here), preferred...  11.6 us
    unnamed x14, local copies, waits for them, and re-layouts  10.9 us
    all_to_all x1, starting transfers between devices, body(): lax.all_to_all(sectioned, ('slot', 'own'), split_axis=0, concat_axis=0, t...  7.3 us
  transfers between devices with their start and end apart: 4, of which 4 were waited for; matrix products, arithmetic and copies ran while one was open for 7% of the time, Pallas kernels for 0%

commit v1 on v0

v1 whole, which is shorter than its diff:
```python
import jax
import jax.numpy as jnp
from jax import lax
from jax.experimental import pallas as pl
from jax.experimental.pallas import tpu as pltpu
from jax.sharding import PartitionSpec as P


def slot_table(counts, n_slots):
    bounds = jnp.cumsum(counts)
    slots = jnp.arange(n_slots, dtype=jnp.int32)
    return jnp.sum((bounds[None, :] <= slots[:, None]).astype(jnp.int32), axis=1)


def update_kernel(first, last, pieces, w, m, v, new_w, new_m, new_v):
    e = pl.program_id(0)
    grad = lax.fori_loop(
        first[e],
        last[e],
        lambda g, acc: acc + pieces[g].astype(jnp.float32),
        jnp.zeros(pieces.shape[1:], jnp.float32),
    )
    moment = 0.9 * m[0] + 0.1 * grad
    second = 0.95 * v[0] + 0.05 * grad * grad
    bias_one = 1.0 - 0.9**10
    bias_two = 1.0 - 0.95**10
    update = 0.001 * (moment / bias_one) / (jnp.sqrt(second / bias_two) + 1e-08)
    new_m[0] = moment
    new_v[0] = second
    new_w[0] = (w[0].astype(jnp.float32) - update).astype(jnp.bfloat16)


def adam(counts_old, pieces, weights, moment, second):
    experts, rows, cols = weights.shape
    last = jnp.cumsum(counts_old)
    first = last - counts_old
    one = pl.BlockSpec((1, rows, cols), lambda e, *_: (e, 0, 0))
    return pl.pallas_call(
        update_kernel,
        grid_spec=pltpu.PrefetchScalarGridSpec(
            num_scalar_prefetch=2,
            grid=(experts,),
            in_specs=[pl.BlockSpec(pieces.shape, lambda e, *_: (0, 0, 0)), one, one, one],
            out_specs=[one, one, one],
        ),
        out_shape=(
            jax.ShapeDtypeStruct(weights.shape, jnp.bfloat16),
            jax.ShapeDtypeStruct(weights.shape, jnp.float32),
            jax.ShapeDtypeStruct(weights.shape, jnp.float32),
        ),
        compiler_params=pltpu.CompilerParams(vmem_limit_bytes=40 * 1024 * 1024),
    )(first, last, pieces, weights, moment, second)


def grouped_kernel(ids, x, w, out):
    e = pl.program_id(0)

    @pl.when(e == 0)
    def _():
        out[...] = jnp.zeros_like(out)

    block = w[:, 0].reshape(x.shape[1], out.shape[1])
    produced = jnp.dot(x[...], block, preferred_element_type=jnp.float32)
    out[...] = jnp.where(ids[...] == e, produced.astype(jnp.bfloat16), out[...])


def grouped(ids, x, gathered):
    parts, experts, rows, cols = gathered.shape
    tokens, hidden = x.shape
    return pl.pallas_call(
        grouped_kernel,
        grid=(experts,),
        in_specs=[
            pl.BlockSpec((tokens, 1), lambda e: (0, 0)),
            pl.BlockSpec((tokens, hidden), lambda e: (0, 0)),
            pl.BlockSpec((parts, 1, rows, cols), lambda e: (0, e, 0, 0)),
        ],
        out_specs=pl.BlockSpec((tokens, cols), lambda e: (0, 0)),
        out_shape=jax.ShapeDtypeStruct((tokens, cols), jnp.bfloat16),
        compiler_params=pltpu.CompilerParams(vmem_limit_bytes=40 * 1024 * 1024),
    )(ids, x, gathered)


def body(slot_grads, weights, moment, second, counts_old, counts_new, inputs, row_slot):
    n_slot = lax.axis_size("slot")
    n_own = lax.axis_size("own")
    devices = n_slot * n_own
    experts, rows_here, cols_here = weights.shape
    table_new = slot_table(counts_new, devices)
    ids_here = jnp.sum(
        jnp.where(row_slot == jnp.arange(devices, dtype=jnp.int32)[None, :], table_new[None, :], 0),
        axis=1,
        keepdims=True,
    )
    ids = lax.all_gather(ids_here, "own", axis=0, tiled=True)
    x = lax.all_gather(inputs, "own", axis=0, tiled=True)
    sectioned = (
        slot_grads.reshape(n_slot, rows_here, n_own, cols_here)
        .transpose(0, 2, 1, 3)
        .reshape(devices, rows_here, cols_here)
    )
    pieces = lax.all_to_all(sectioned, ("slot", "own"), split_axis=0, concat_axis=0, tiled=True)
    new_weights, new_moment, new_second = adam(counts_old, pieces, weights, moment, second)
    gathered = lax.all_gather(new_weights, "slot", axis=0, tiled=False)
    produced = grouped(ids, x, gathered)
    outputs = lax.all_to_all(produced, "own", split_axis=0, concat_axis=1, tiled=True)
    return (new_weights, new_moment, new_second, outputs)


def solution(mesh):
    whole = P(None, "slot", "own")
    by_slot = P(("slot", "own"), None)
    return jax.shard_map(
        body,
        mesh=mesh,
        in_specs=(P(("slot", "own"), None, None), whole, whole, whole, P(), P(), by_slot, by_slot),
        out_specs=(whole, whole, whole, by_slot),
        check_vma=False,
    )
```

time: 260 us -> 261 us (level)
  blocking collectives: 0 us -> 42.6 us
  waiting for transfers between devices: 189 us -> 154 us
  Pallas kernels: 0 us -> 26.9 us
  matrix products: 15.9 us -> 0 us
  starting transfers between devices: 21.7 us -> 7.38 us
  local copies, waits for them, and re-layouts: 29.4 us -> 15.4 us
  between operations: 0.78 us -> 14.1 us
    all_to_all x3 -> x0, waiting for transfers between devices: 121 us -> none  [the longest x1 66.2 us: body(): lax.all_to_all(hosted, ('slot', 'own'), split_axis=0, concat_axis=0, tile...]
    all_gather x0 -> x2, waiting for transfers between devices: none -> 60.1 us  [the longest x1 60.1 us: body(): gathered = lax.all_gather(new_weights, 'slot', axis=0, tiled=False)]
    all_to_all x0 -> x1, blocking collectives: none -> 30.6 us  [body(): lax.all_to_all(produced, 'own', split_axis=0, concat_axis=1, tiled=True)]
    pallas_call x0 -> x2, Pallas kernels: none -> 26.9 us  [the longest x1 18.2 us: grouped(): pl.pallas_call(grouped_kernel, grid=(experts,), in_specs=[pl.BlockSpec((t...]
    all_to_all x1, waiting for transfers between devices: 68.8 us -> 92.8 us  [body(): lax.all_to_all(sectioned, ('slot', 'own'), split_axis=0, concat_axis=0, t...]
    dot_general x2 -> x0, matrix products: 15.9 us -> none  [the longest x1 11.6 us: body(): jnp.dot(select, pieces.reshape(devices, rows_here * cols_here), preferred...]
    all_to_all x3 -> x0, starting transfers between devices: 14.4 us -> none  [the longest x1 5.15 us: body(): lax.all_to_all(outgoing.reshape(devices, capacity, hidden), ('slot', 'own...]
    all_gather x0 -> x1, blocking collectives: none -> 12.1 us  [body(): ids = lax.all_gather(ids_here, 'own', axis=0, tiled=True)]
  transfers between devices with their start and end apart: 4 -> 3, of which waited for: 4 -> 2; matrix products, arithmetic and copies ran while one was open for 7% -> 0% of each run, Pallas kernels for 0% -> 3%
where the time goes in v1:
time: 261 us; the launch traced here: 260 us
  waiting for transfers between devices  154 us (59%)
  blocking collectives  42.6 us (16%)
  Pallas kernels  26.9 us (10%)
  local copies, waits for them, and re-layouts  15.4 us (6%)
  between operations  14.1 us (5%)
  starting transfers between devices  7.38 us (3%)
    all_to_all x1, waiting for transfers between devices, body(): lax.all_to_all(sectioned, ('slot', 'own'), split_axis=0, concat_axis=0, t...  92.8 us
    all_gather x1, waiting for transfers between devices, body(): gathered = lax.all_gather(new_weights, 'slot', axis=0, tiled=False)  60.1 us
    all_to_all x1, blocking collectives, body(): lax.all_to_all(produced, 'own', split_axis=0, concat_axis=1, tiled=True)  30.6 us
    pallas_call x1, Pallas kernels, grouped(): pl.pallas_call(grouped_kernel, grid=(experts,), in_specs=[pl.BlockSpec((t...  18.2 us
    all_gather x1, blocking collectives, body(): ids = lax.all_gather(ids_here, 'own', axis=0, tiled=True)  12.1 us
    pallas_call x1, Pallas kernels, adam(): pl.pallas_call(update_kernel, grid_spec=pltpu.PrefetchScalarGridSpec(num_...  8.64 us
    all_to_all x1, starting transfers between devices, body(): lax.all_to_all(sectioned, ('slot', 'own'), split_axis=0, concat_axis=0, t...  7.3 us
    reshape x2, local copies, waits for them, and re-layouts, body(): slot_grads.reshape(n_slot, rows_here, n_own, cols_here)  7.26 us
  transfers between devices with their start and end apart: 3, of which 2 were waited for; matrix products, arithmetic and copies ran while one was open for 0% of the time, Pallas kernels for 3%

profile of v1, /device:TPU:0, one launch (start us, length us, event | category | flops | bytes accessed | tf_op | source)
XLA Modules:
  0.0 260.4 jit_solution(7985784433412129378)
XLA Ops:
  7.2 4.8 %reshape.70 = bf16[8,96,4,512]{3,2,1,0:T(4,128)(2,1)S(1)} reshape(bf16[1,768,2048]{2,1,0:T(8,128)(2,1)} %param.8) | data formatting | bytes 6291456 | tf_op jit(solution)/shard_map/reshape | solution.py:98
  12.0 2.5 copy.27
  14.4 0.0 copy-start.5
  14.4 7.3 %all-to-all-start = ((bf16[32,96,512]{2,1,0:T(8,128)(2,1)}), bf16[32,96,512]{2,1,0:T(8,128)(2,1)S(1)}, u32[]{:S(2)}, u32[]{:S(2)}) async-start(bf16[32,96,512]{2,1,0:T(8,128)(2,1)} %bitcast.14), calls=%async_computation | async-start | bytes 6291456 | tf_op jit(solution)/shard_map/all_to_all | solution.py:102
  21.7 0.0 all-gather.6.cloned.1.call-start
  21.8 0.7 all-gather.6.cloned.1.call-update
  22.5 0.0 all-gather.8.cloned.1.call-start
  22.5 0.0 copy-done.5
  22.5 0.1 copy.26
  22.7 0.1 reduce.last
  22.8 92.8 %all-to-all-done.pieces = bf16[32,96,512]{2,1,0:T(8,128)(2,1)S(1)} async-done(((bf16[32,96,512]{2,1,0:T(8,128)(2,1)}), bf16[32,96,512]{2,1,0:T(8,128)(2,1)S(1)}, u32[]{:S(2)}, u32[]{:S(2)}) %all-to-all-start) | async-done | bytes 3145760 | tf_op jit(solution)/shard_map/all_to_all | solution.py:102
  115.6 0.0 copy-start
  115.6 1.9 copy-done
  117.5 0.0 copy-start.1
  117.5 1.9 copy-done.1
  119.4 0.0 copy-start.2
  119.4 1.4 copy-done.2
  120.8 0.0 copy-start.6
  120.8 0.0 copy-start.4
  120.8 8.6 %shard_map.111 = (bf16[16,96,512]{2,1,0:T(8,128)(2,1)}, f32[16,96,512]{2,1,0:T(8,128)}, f32[16,96,512]{2,1,0:T(8,128)}) custom-call(s32[16]{0:T(128)S(1)} %sub.3.first, s32[16]{0:T(128)S(1)} %reduce.last, bf16[32,96,512]{2,1,0:T(8,128)(2,1)S(1)} %all-to-all-done.pieces, bf16[16,96,512]{2,1,0:T(8,128)(2,1)S(1)} %copy-done.2, f32[16,96,512]{2,1,0:T(8,128)S(1)} %copy-done, ...), custom_call_target="tpu_custom_call" | custom-call | tf_op jit(solution)/shard_map/pallas_call | solution.py:38
  129.4 0.0 all-gather.8.cloned.1.call-update
  129.5 0.0 copy-done.6
  129.5 0.1 copy.28
  129.6 0.1 reduce.1
  129.7 0.1 convert_reduce_fusion
  129.8 0.0 copy-done.4
  129.8 0.1 select_reduce_fusion
  129.9 12.1 %all-gather.2 = s32[4,1,256]{2,1,0:T(1,128)S(1)} all-gather(s32[1,1,256]{2,1,0:T(1,128)S(1)} %bitcast.19), channel_id=2, replica_groups=mesh['slot'=8,'own'=4] {'own'}, dimensions={0}, use_global_device_ids=true | all-gather | bytes 5120 | tf_op jit(solution)/shard_map/all_gather | solution.py:95
  142.0 0.2 copy.29.ids
  142.2 0.0 all-gather.6.cloned.1.call-done.x
  142.2 60.1 %all-gather.8.cloned.1.call-done = bf16[128,96,512]{2,1,0:T(8,128)(2,1)} async-done(((bf16[16,96,512]{2,1,0:T(8,128)(2,1)}), bf16[128,96,512]{2,1,0:T(8,128)(2,1)}) %all-gather.8.cloned.1.call-update) | async-done | bytes 12582928 | tf_op jit(solution)/shard_map/all_gather | solution.py:104
  202.3 0.0 copy-start.3
  202.3 1.4 copy-done.3
  203.7 18.2 %shard_map.112 = bf16[1024,512]{1,0:T(8,128)(2,1)S(1)} custom-call(s32[1024,1]{1,0:T(8,128)S(1)} %copy.29.ids, bf16[1024,768]{1,0:T(8,128)(2,1)S(1)} %copy-done.3, bf16[8,16,96,512]{3,2,1,0:T(8,128)(2,1)} %bitcast.15), custom_call_target="tpu_custom_call" | custom-call | tf_op jit(solution)/shard_map/pallas_call | solution.py:70
  221.9 30.6 %all_to_all.24 = bf16[4,256,512]{2,1,0:T(8,128)(2,1)S(1)} all-to-all(bf16[4,256,512]{2,1,0:T(8,128)(2,1)S(1)} %bitcast.13), channel_id=1, replica_groups=mesh['slot'=8,'own'=4] {'own'}, dimensions={0} | all-to-all | bytes 2097152 | tf_op jit(solution)/shard_map/all_to_all | solution.py:106
  252.5 1.1 copy.31
  (3 shorter events, 0.1 us)
Async XLA Ops:
  14.4 8.1 %copy-start.5 = (s32[16]{0:T(128)S(1)}, s32[16]{0:T(128)}, u32[]{:S(2)}) copy-start(s32[16]{0:T(128)} %param.12) | copy-start | bytes 196
  14.4 101.2 %all-to-all-start = ((bf16[32,96,512]{2,1,0:T(8,128)(2,1)}), bf16[32,96,512]{2,1,0:T(8,128)(2,1)S(1)}, u32[]{:S(2)}, u32[]{:S(2)}) async-start(bf16[32,96,512]{2,1,0:T(8,128)(2,1)} %bitcast.14), calls=%async_computation | async-start | bytes 6291456 | tf_op jit(solution)/shard_map/all_to_all | solution.py:102
  21.7 120.5 %all-gather.6.cloned.1.call-start = ((), (), s32[]{:S(2)}) async-start(), calls=%async_computation.2 | async-start | bytes 1966080 | tf_op jit(solution)/shard_map/all_gather | solution.py:96
  22.5 179.8 %all-gather.8.cloned.1.call-start = ((), (), s32[]{:S(2)}) async-start(), calls=%async_computation.3 | async-start | bytes 14155776 | tf_op jit(solution)/shard_map/all_gather | solution.py:104
  115.6 1.9 copy-start
  117.5 1.9 copy-start.1
  119.4 1.4 copy-start.2
  120.8 8.7 %copy-start.6 = (s32[16]{0:T(128)S(1)}, s32[16]{0:T(128)}, u32[]{:S(2)}) copy-start(s32[16]{0:T(128)} %param.13) | copy-start | bytes 196
  120.8 9.0 %copy-start.4 = (s32[256,1]{0,1:T(1,128)S(1)}, s32[256,1]{0,1:T(1,128)}, u32[]{:S(2)}) copy-start(s32[256,1]{0,1:T(1,128)} %param.15) | copy-start | bytes 3076
  202.3 1.4 copy-start.3
Sparse Core Ops, SparseCore 0:
  24.1 78.7 all-gather.5
  129.6 72.6 all-gather.7

commit v2 on v1

--- a/solution.py
+++ b/solution.py
@@ -1,3 +1,5 @@
+import functools
+
 import jax
 import jax.numpy as jnp
 from jax import lax
@@ -48,37 +50,201 @@
             jax.ShapeDtypeStruct(weights.shape, jnp.float32),
             jax.ShapeDtypeStruct(weights.shape, jnp.float32),
         ),
-        compiler_params=pltpu.CompilerParams(vmem_limit_bytes=40 * 1024 * 1024),
+        compiler_params=pltpu.CompilerParams(vmem_limit_bytes=58 * 1024 * 1024),
     )(first, last, pieces, weights, moment, second)
 
 
-def grouped_kernel(ids, x, w, out):
-    e = pl.program_id(0)
-
-    @pl.when(e == 0)
-    def _():
-        out[...] = jnp.zeros_like(out)
-
-    block = w[:, 0].reshape(x.shape[1], out.shape[1])
-    produced = jnp.dot(x[...], block, preferred_element_type=jnp.float32)
-    out[...] = jnp.where(ids[...] == e, produced.astype(jnp.bfloat16), out[...])
-
-
-def grouped(ids, x, gathered):
-    parts, experts, rows, cols = gathered.shape
-    tokens, hidden = x.shape
+CHUNKS = 8
+MESH = pl.DeviceIdType.MESH
+
+
+def bit_orders(n_slot):
+    bits = n_slot.bit_length() - 1
+    between = list(range(1, bits))
+    half = len(between) // 2
+    return between + [0], between[half:] + between[:half] + [0]
+
+
+def flip(index, mask):
+    bit = 1
+    while bit <= mask:
+        if mask & bit:
+            index = index + bit - 2 * bit * lax.rem(lax.div(index, bit), 2)
+        bit *= 2
+    return index
+
+
+def expert_kernel(
+    n_slot, n_own, x_here, w_here, out, store, x_all, held, y, out_sems, load_sems, local_sems, x_send, x_recv, w_send, w_recv, y_send, y_recv
+):
+    slot = lax.axis_index("slot")
+    own = lax.axis_index("own")
+    tok, width = x_here.shape
+    experts, rows, cols = w_here.shape
+    hidden = n_slot * rows
+    per = experts // CHUNKS
+    orders = bit_orders(n_slot)
+    bits = len(orders[0])
+
+    partners = [(flip(slot, 1 << b), own) for b in range(bits)]
+    partners += [(slot, lax.rem(own + k, n_own)) for k in range(1, n_own)]
+    barrier = pltpu.get_barrier_semaphore()
+    for partner in partners:
+        pl.semaphore_signal(barrier, inc=1, device_id=partner, device_id_type=MESH)
+    pl.semaphore_wait(barrier, len(partners))
+
+    def step_copies(chunk, step):
+        order = orders[chunk % 2]
+        group = pl.ds(chunk * per, per)
+        sources = [0]
+        for b in order[:step]:
+            sources = sources + [o ^ (1 << b) for o in sources]
+        copies = []
+        for i, offset in enumerate(sources):
+            n = (1 << step) - 1 + i
+            origin = flip(slot, offset)
+            source = w_here.at[group] if offset == 0 else store.at[origin, group]
+            copies.append(
+                pltpu.make_async_remote_copy(
+                    src_ref=source,
+                    dst_ref=store.at[origin, group],
+                    send_sem=w_send.at[chunk, n],
+                    recv_sem=w_recv.at[chunk, n],
+                    device_id=(flip(slot, 1 << order[step]), own),
+                    device_id_type=MESH,
+                )
+            )
+        return copies
+
+    steps = [[step_copies(c, k) for k in range(bits)] for c in range(CHUNKS)]
+    for c in range(CHUNKS):
+        for copy in steps[c][0]:
+            copy.start()
+    x_copies = [
+        pltpu.make_async_remote_copy(
+            src_ref=x_here,
+            dst_ref=x_all.at[own],
+            send_sem=x_send.at[k],
+            recv_sem=x_recv.at[k],
+            device_id=(slot, lax.rem(own + k, n_own)),
+            device_id_type=MESH,
+        )
+        for k in range(1, n_own)
+    ]
+    for copy in x_copies:
+        copy.start()
+    x_mine = pltpu.make_async_copy(x_here, x_all.at[own], local_sems.at[0])
+    x_mine.start()
+    w_mine = pltpu.make_async_copy(w_here, store.at[slot], local_sems.at[1])
+    w_mine.start()
+    y[...] = jnp.zeros_like(y)
+
+    def load(chunk):
+        return pltpu.make_async_copy(
+            store.at[:, pl.ds(chunk * per, per)], held.at[chunk % 2], load_sems.at[chunk % 2]
+        )
+
+    def product(chunk, at, block):
+        weight = held[chunk % 2, :, at].reshape(hidden, cols)
+        ids = x_all[block, :, hidden : hidden + 1].astype(jnp.float32)
+        number = (chunk * per + at).astype(jnp.float32)
+        made = jnp.dot(x_all[block, :, :hidden], weight, preferred_element_type=jnp.float32)
+        y[block] = jnp.where(ids == number, made.astype(jnp.bfloat16), y[block])
+
+    y_copies = []
+
+    def compute(chunk):
+        load(chunk).wait()
+        if chunk < CHUNKS - 1:
+            def one(i, _):
+                product(chunk, lax.div(i, n_own), lax.rem(i, n_own))
+                return 0
+
+            lax.fori_loop(0, per * n_own, one, 0)
+            return
+        for k in [n_own // 2 + j for j in range(n_own - n_own // 2)] + list(range(1, n_own // 2)) + [0]:
+            block = lax.rem(own + k, n_own)
+
+            def one(i, _):
+                product(chunk, i, block)
+                return 0
+
+            lax.fori_loop(0, per, one, 0)
+            target = out.at[:, pl.ds(pl.multiple_of(own * cols, cols), cols)]
+            if k == 0:
+                copy = pltpu.make_async_copy(y.at[block], target, out_sems.at[0])
+            else:
+                copy = pltpu.make_async_remote_copy(
+                    src_ref=y.at[block],
+                    dst_ref=target,
+                    send_sem=y_send.at[k],
+                    recv_sem=y_recv.at[k],
+                    device_id=(slot, block),
+                    device_id_type=MESH,
+                )
+            copy.start()
+            y_copies.append(copy)
+
+    for tick in range(CHUNKS + bits + 1):
+        for k in range(bits):
+            c = tick - k
+            if 0 <= c < CHUNKS:
+                for copy in steps[c][k]:
+                    copy.wait_recv()
+                if k + 1 < bits:
+                    for copy in steps[c][k + 1]:
+                        copy.start()
+        c = tick - (bits - 1)
+        if c == 0:
+            w_mine.wait()
+            x_mine.wait()
+            for copy in x_copies:
+                copy.wait_recv()
+        if 0 <= c < CHUNKS:
+            load(c).start()
+        if 0 <= c - 1 < CHUNKS:
+            compute(c - 1)
+    for c in range(CHUNKS):
+        for k in range(bits):
+            for copy in steps[c][k]:
+                copy.wait_send()
+    for copy in x_copies:
+        copy.wait_send()
+    for copy in y_copies:
+        copy.wait()
+
+
+def expert_rows(n_slot, n_own, x_here, new_weights):
+    tok, width = x_here.shape
+    experts, rows, cols = new_weights.shape
+    hbm = pl.BlockSpec(memory_space=pl.ANY)
+    dma = pltpu.SemaphoreType.DMA
     return pl.pallas_call(
-        grouped_kernel,
-        grid=(experts,),
-        in_specs=[
-            pl.BlockSpec((tokens, 1), lambda e: (0, 0)),
-            pl.BlockSpec((tokens, hidden), lambda e: (0, 0)),
-            pl.BlockSpec((parts, 1, rows, cols), lambda e: (0, e, 0, 0)),
+        functools.partial(expert_kernel, n_slot, n_own),
+        in_specs=[hbm, hbm],
+        out_specs=[hbm, hbm],
+        out_shape=(
+            jax.ShapeDtypeStruct((tok, n_own * cols), jnp.bfloat16),
+            jax.ShapeDtypeStruct((n_slot, experts, rows, cols), jnp.bfloat16),
+        ),
+        scratch_shapes=[
+            pltpu.VMEM((n_own, tok, width), jnp.bfloat16),
+            pltpu.VMEM((2, n_slot, experts // CHUNKS, rows, cols), jnp.bfloat16),
+            pltpu.VMEM((n_own, tok, cols), jnp.bfloat16),
+            dma((1,)),
+            dma((2,)),
+            dma((2,)),
+            dma((n_own,)),
+            dma((n_own,)),
+            dma((CHUNKS, n_slot - 1)),
+            dma((CHUNKS, n_slot - 1)),
+            dma((n_own,)),
+            dma((n_own,)),
         ],
-        out_specs=pl.BlockSpec((tokens, cols), lambda e: (0, 0)),
-        out_shape=jax.ShapeDtypeStruct((tokens, cols), jnp.bfloat16),
-        compiler_params=pltpu.CompilerParams(vmem_limit_bytes=40 * 1024 * 1024),
-    )(ids, x, gathered)
+        compiler_params=pltpu.CompilerParams(
+            collective_id=0, has_side_effects=True, vmem_limit_bytes=58 * 1024 * 1024
+        ),
+    )(x_here, new_weights)[0]
 
 
 def body(slot_grads, weights, moment, second, counts_old, counts_new, inputs, row_slot):
@@ -92,8 +258,8 @@
         axis=1,
         keepdims=True,
     )
-    ids = lax.all_gather(ids_here, "own", axis=0, tiled=True)
-    x = lax.all_gather(inputs, "own", axis=0, tiled=True)
+    marks = jnp.broadcast_to(ids_here, (inputs.shape[0], 128)).astype(jnp.bfloat16)
+    x_here = jnp.concatenate([inputs, marks], axis=1)
     sectioned = (
         slot_grads.reshape(n_slot, rows_here, n_own, cols_here)
         .transpose(0, 2, 1, 3)
@@ -101,9 +267,7 @@
     )
     pieces = lax.all_to_all(sectioned, ("slot", "own"), split_axis=0, concat_axis=0, tiled=True)
     new_weights, new_moment, new_second = adam(counts_old, pieces, weights, moment, second)
-    gathered = lax.all_gather(new_weights, "slot", axis=0, tiled=False)
-    produced = grouped(ids, x, gathered)
-    outputs = lax.all_to_all(produced, "own", split_axis=0, concat_axis=1, tiled=True)
+    outputs = expert_rows(n_slot, n_own, x_here, new_weights)
     return (new_weights, new_moment, new_second, outputs)
 
 

time: 261 us -> 223 us (0.85)
  Pallas kernels: 26.9 us -> 131 us
  waiting for transfers between devices: 154 us -> 64.9 us
  blocking collectives: 42.6 us -> 0 us
  between operations: 14.1 us -> 0.69 us
  other arithmetic: 0.5 us -> 3.63 us
    pallas_call x1, Pallas kernels: 18.2 us -> 117 us  [expert_rows(): pl.pallas_call(functools.partial(expert_kernel, n_slot, n_own), in_specs=...]
    all_gather x2 -> x0, waiting for transfers between devices: 60.1 us -> none  [the longest x1 60.1 us: body(): gathered = lax.all_gather(new_weights, 'slot', axis=0, tiled=False)]
    all_to_all x1 -> x0, blocking collectives: 30.6 us -> none  [body(): lax.all_to_all(produced, 'own', split_axis=0, concat_axis=1, tiled=True)]
    all_to_all x1, waiting for transfers between devices: 92.8 us -> 64.9 us  [body(): lax.all_to_all(sectioned, ('slot', 'own'), split_axis=0, concat_axis=0, t...]
    all_gather x1 -> x0, blocking collectives: 12.1 us -> none  [body(): ids = lax.all_gather(ids_here, 'own', axis=0, tiled=True)]
    pallas_call x1, Pallas kernels: 8.64 us -> 14.8 us  [adam(): pl.pallas_call(update_kernel, grid_spec=pltpu.PrefetchScalarGridSpec(num_...]
    unnamed x14 -> x9, local copies, waits for them, and re-layouts: 6.6 us -> 3.98 us
  transfers between devices with their start and end apart: 3 -> 1, of which waited for: 2 -> 1; matrix products, arithmetic and copies ran while one was open for 0% -> 2% of each run, Pallas kernels for 3% -> 0%
where the time goes in v2:
time: 223 us; the launch traced here: 221 us
  Pallas kernels  131 us (59%)
  waiting for transfers between devices  64.9 us (29%)
  local copies, waits for them, and re-layouts  12.8 us (6%)
  starting transfers between devices  7.3 us (3%)
  other arithmetic  3.63 us (2%)
    pallas_call x1, Pallas kernels, expert_rows(): pl.pallas_call(functools.partial(expert_kernel, n_slot, n_own), in_specs=...  117 us
    all_to_all x1, waiting for transfers between devices, body(): lax.all_to_all(sectioned, ('slot', 'own'), split_axis=0, concat_axis=0, t...  64.9 us
    pallas_call x1, Pallas kernels, adam(): pl.pallas_call(update_kernel, grid_spec=pltpu.PrefetchScalarGridSpec(num_...  14.8 us
    all_to_all x1, starting transfers between devices, body(): lax.all_to_all(sectioned, ('slot', 'own'), split_axis=0, concat_axis=0, t...  7.3 us
    reshape x2, local copies, waits for them, and re-layouts, body(): slot_grads.reshape(n_slot, rows_here, n_own, cols_here)  7.26 us
  transfers between devices with their start and end apart: 1, of which 1 were waited for; matrix products, arithmetic and copies ran while one was open for 2% of the time, Pallas kernels for 0%

profile of v2, /device:TPU:0, one launch (start us, length us, event | category | flops | bytes accessed | tf_op | source)
XLA Modules:
  0.0 220.7 jit_solution(5436794629120970779)
XLA Ops:
  0.6 4.8 %reshape.68 = bf16[8,96,4,512]{3,2,1,0:T(4,128)(2,1)S(1)} reshape(bf16[1,768,2048]{2,1,0:T(8,128)(2,1)} %param.8) | data formatting | bytes 6291456 | tf_op jit(solution)/shard_map/reshape | solution.py:264
  5.4 2.5 %copy.19 = bf16[8,96,4,512]{3,1,2,0:T(8,128)(2,1)} copy(bf16[8,96,4,512]{3,2,1,0:T(4,128)(2,1)S(1)} %reshape.68) | data formatting | bytes 6291456 | tf_op jit(solution)/shard_map/reshape | solution.py:264
  7.9 0.0 copy-start.3
  7.9 0.0 copy-start.1
  7.9 7.3 %all-to-all-start = ((bf16[32,96,512]{2,1,0:T(8,128)(2,1)}), bf16[32,96,512]{2,1,0:T(8,128)(2,1)S(1)}, u32[]{:S(2)}, u32[]{:S(2)}) async-start(bf16[32,96,512]{2,1,0:T(8,128)(2,1)} %bitcast.2), calls=%async_computation | async-start | bytes 6291456 | tf_op jit(solution)/shard_map/all_to_all | solution.py:268
  15.2 0.0 copy-done.3
  15.2 0.1 copy.20
  15.3 0.1 reduce.1
  15.5 0.1 convert_reduce_fusion
  15.6 0.8 select_reduce_fusion
  16.3 0.5 convert_element_type.8
  16.8 0.7 copy.18
  17.6 0.1 reduce.last
  17.7 0.0 copy-start.2
  17.7 1.1 sub.3.first
  18.9 0.7 broadcast_in_dim.24
  19.6 0.0 copy-done.1
  19.6 0.8 pad_maximum_fusion.x_here
  20.4 64.9 %all-to-all-done.pieces = bf16[32,96,512]{2,1,0:T(8,128)(2,1)S(1)} async-done(((bf16[32,96,512]{2,1,0:T(8,128)(2,1)}), bf16[32,96,512]{2,1,0:T(8,128)(2,1)S(1)}, u32[]{:S(2)}, u32[]{:S(2)}) %all-to-all-start) | async-done | bytes 3145760 | tf_op jit(solution)/shard_map/all_to_all | solution.py:268
  85.4 0.0 copy-done.2
  85.4 0.0 copy-start
  85.4 1.7 copy-done
  87.0 14.8 %shard_map.111 = (bf16[16,96,512]{2,1,0:T(8,128)(2,1)}, f32[16,96,512]{2,1,0:T(8,128)}, f32[16,96,512]{2,1,0:T(8,128)}) custom-call(s32[16]{0:T(128)} %sub.3.first, s32[16]{0:T(128)} %copy-done.2, bf16[32,96,512]{2,1,0:T(8,128)(2,1)} %copy-done, bf16[16,96,512]{2,1,0:T(8,128)(2,1)} %w.1, f32[16,96,512]{2,1,0:T(8,128)} %m.1, f32[16,96,512]{2,1,0:T(8,128)} %v.1), custom_call_target="tpu_custom_call" | custom-call | tf_op jit(solution)/shard_map/pallas_call | solution.py:40
  101.8 116.6 %shard_map.112 = (bf16[256,2048]{1,0:T(8,128)(2,1)}, bf16[8,16,96,512]{3,2,1,0:T(8,128)(2,1)}) custom-call(bf16[256,896]{1,0:T(8,128)(2,1)} %pad_maximum_fusion.x_here, bf16[16,96,512]{2,1,0:T(8,128)(2,1)} %get-tuple-element.16.w_here), custom_call_target="tpu_custom_call" | custom-call | tf_op jit(solution)/shard_map/pallas_call | solution.py:222
  218.4 2.3 %copy.22 = bf16[256,2048]{1,0:T(8,128)(2,1)} copy(bf16[256,2048]{1,0:T(8,128)(2,1)} %get-tuple-element.19) | data formatting | bytes 2097152
  (2 shorter events, 0.1 us)
Async XLA Ops:
  7.9 7.3 %copy-start.3 = (s32[16]{0:T(128)S(1)}, s32[16]{0:T(128)}, u32[]{:S(2)}) copy-start(s32[16]{0:T(128)} %param.13) | copy-start | bytes 196
  7.9 11.7 %copy-start.1 = (bf16[256,768]{1,0:T(8,128)(2,1)S(1)}, bf16[256,768]{1,0:T(8,128)(2,1)}, u32[]{:S(2)}) copy-start(bf16[256,768]{1,0:T(8,128)(2,1)} %param.14) | copy-start | bytes 1179652
  7.9 77.5 %all-to-all-start = ((bf16[32,96,512]{2,1,0:T(8,128)(2,1)}), bf16[32,96,512]{2,1,0:T(8,128)(2,1)S(1)}, u32[]{:S(2)}, u32[]{:S(2)}) async-start(bf16[32,96,512]{2,1,0:T(8,128)(2,1)} %bitcast.2), calls=%async_computation | async-start | bytes 6291456 | tf_op jit(solution)/shard_map/all_to_all | solution.py:268
  17.7 67.7 %copy-start.2 = (s32[16]{0:T(128)}, s32[16]{0:T(128)S(1)}, u32[]{:S(2)}) copy-start(s32[16]{0:T(128)S(1)} %reduce.last) | copy-start | bytes 196
  85.4 1.7 copy-start

commit v3 on v2

--- a/solution.py
+++ b/solution.py
@@ -54,7 +54,10 @@
     )(first, last, pieces, weights, moment, second)
 
 
-CHUNKS = 8
+HALVES = 2
+GROUPS = 4
+CHUNKS = HALVES * GROUPS
+LAG = 2
 MESH = pl.DeviceIdType.MESH
 
 
@@ -82,7 +85,8 @@
     tok, width = x_here.shape
     experts, rows, cols = w_here.shape
     hidden = n_slot * rows
-    per = experts // CHUNKS
+    per = experts // GROUPS
+    wide = cols // HALVES
     orders = bit_orders(n_slot)
     bits = len(orders[0])
 
@@ -95,7 +99,8 @@
 
     def step_copies(chunk, step):
         order = orders[chunk % 2]
-        group = pl.ds(chunk * per, per)
+        group = pl.ds(chunk % GROUPS * per, per)
+        part = pl.ds(chunk // GROUPS * wide, wide)
         sources = [0]
         for b in order[:step]:
             sources = sources + [o ^ (1 << b) for o in sources]
@@ -103,11 +108,11 @@
         for i, offset in enumerate(sources):
             n = (1 << step) - 1 + i
             origin = flip(slot, offset)
-            source = w_here.at[group] if offset == 0 else store.at[origin, group]
+            source = w_here.at[group, :, part] if offset == 0 else store.at[origin, group, :, part]
             copies.append(
                 pltpu.make_async_remote_copy(
                     src_ref=source,
-                    dst_ref=store.at[origin, group],
+                    dst_ref=store.at[origin, group, :, part],
                     send_sem=w_send.at[chunk, n],
                     recv_sem=w_recv.at[chunk, n],
                     device_id=(flip(slot, 1 << order[step]), own),
@@ -141,21 +146,23 @@
 
     def load(chunk):
         return pltpu.make_async_copy(
-            store.at[:, pl.ds(chunk * per, per)], held.at[chunk % 2], load_sems.at[chunk % 2]
+            store.at[:, pl.ds(chunk % GROUPS * per, per), :, pl.ds(chunk // GROUPS * wide, wide)], held.at[chunk % 2], load_sems.at[chunk % 2]
         )
 
     def product(chunk, at, block):
-        weight = held[chunk % 2, :, at].reshape(hidden, cols)
+        weight = held[chunk % 2, :, at].reshape(hidden, wide)
         ids = x_all[block, :, hidden : hidden + 1].astype(jnp.float32)
-        number = (chunk * per + at).astype(jnp.float32)
+        number = (chunk % GROUPS * per + at).astype(jnp.float32)
         made = jnp.dot(x_all[block, :, :hidden], weight, preferred_element_type=jnp.float32)
-        y[block] = jnp.where(ids == number, made.astype(jnp.bfloat16), y[block])
+        half = chunk // GROUPS
+        y[half, block] = jnp.where(ids == number, made.astype(jnp.bfloat16), y[half, block])
 
     y_copies = []
 
     def compute(chunk):
         load(chunk).wait()
-        if chunk < CHUNKS - 1:
+        half = chunk // GROUPS
+        if chunk % GROUPS < GROUPS - 1:
             def one(i, _):
                 product(chunk, lax.div(i, n_own), lax.rem(i, n_own))
                 return 0
@@ -170,31 +177,31 @@
                 return 0
 
             lax.fori_loop(0, per, one, 0)
-            target = out.at[:, pl.ds(pl.multiple_of(own * cols, cols), cols)]
+            target = out.at[:, pl.ds(pl.multiple_of(own * cols + half * wide, wide), wide)]
             if k == 0:
-                copy = pltpu.make_async_copy(y.at[block], target, out_sems.at[0])
+                copy = pltpu.make_async_copy(y.at[half, block], target, out_sems.at[half])
             else:
                 copy = pltpu.make_async_remote_copy(
-                    src_ref=y.at[block],
+                    src_ref=y.at[half, block],
                     dst_ref=target,
-                    send_sem=y_send.at[k],
-                    recv_sem=y_recv.at[k],
+                    send_sem=y_send.at[half, k],
+                    recv_sem=y_recv.at[half, k],
                     device_id=(slot, block),
                     device_id_type=MESH,
                 )
             copy.start()
             y_copies.append(copy)
 
-    for tick in range(CHUNKS + bits + 1):
+    for tick in range(CHUNKS + LAG * (bits - 1) + 1):
         for k in range(bits):
-            c = tick - k
+            c = tick - LAG * k
             if 0 <= c < CHUNKS:
                 for copy in steps[c][k]:
                     copy.wait_recv()
                 if k + 1 < bits:
                     for copy in steps[c][k + 1]:
                         copy.start()
-        c = tick - (bits - 1)
+        c = tick - LAG * (bits - 1)
         if c == 0:
             w_mine.wait()
             x_mine.wait()
@@ -229,17 +236,17 @@
         ),
         scratch_shapes=[
             pltpu.VMEM((n_own, tok, width), jnp.bfloat16),
-            pltpu.VMEM((2, n_slot, experts // CHUNKS, rows, cols), jnp.bfloat16),
-            pltpu.VMEM((n_own, tok, cols), jnp.bfloat16),
-            dma((1,)),
+            pltpu.VMEM((2, n_slot, experts // GROUPS, rows, cols // HALVES), jnp.bfloat16),
+            pltpu.VMEM((HALVES, n_own, tok, cols // HALVES), jnp.bfloat16),
+            dma((HALVES,)),
             dma((2,)),
             dma((2,)),
             dma((n_own,)),
             dma((n_own,)),
             dma((CHUNKS, n_slot - 1)),
             dma((CHUNKS, n_slot - 1)),
-            dma((n_own,)),
-            dma((n_own,)),
+            dma((HALVES, n_own)),
+            dma((HALVES, n_own)),
         ],
         compiler_params=pltpu.CompilerParams(
             collective_id=0, has_side_effects=True, vmem_limit_bytes=58 * 1024 * 1024

time: 223 us -> 205 us (0.919)
  Pallas kernels: 131 us -> 115 us
    pallas_call x1, Pallas kernels: 117 us -> 101 us  [expert_rows(): pl.pallas_call(functools.partial(expert_kernel, n_slot, n_own), in_specs=...]
  transfers between devices with their start and end apart: 1 -> 1, of which waited for: 1 -> 1; matrix products, arithmetic and copies ran while one was open for 2% -> 3% of each run, Pallas kernels for 0% -> 0%
where the time goes in v3:
time: 205 us
  Pallas kernels  115 us (56%)
  waiting for transfers between devices  64.9 us (32%)
  local copies, waits for them, and re-layouts  12.8 us (6%)
  starting transfers between devices  7.3 us (4%)
  other arithmetic  3.63 us (2%)
    pallas_call x1, Pallas kernels, expert_rows(): pl.pallas_call(functools.partial(expert_kernel, n_slot, n_own), in_specs=...  101 us
    all_to_all x1, waiting for transfers between devices, body(): lax.all_to_all(sectioned, ('slot', 'own'), split_axis=0, concat_axis=0, t...  64.9 us
    pallas_call x1, Pallas kernels, adam(): pl.pallas_call(update_kernel, grid_spec=pltpu.PrefetchScalarGridSpec(num_...  14.7 us
    all_to_all x1, starting transfers between devices, body(): lax.all_to_all(sectioned, ('slot', 'own'), split_axis=0, concat_axis=0, t...  7.3 us
    reshape x2, local copies, waits for them, and re-layouts, body(): slot_grads.reshape(n_slot, rows_here, n_own, cols_here)  7.26 us
  transfers between devices with their start and end apart: 1, of which 1 were waited for; matrix products, arithmetic and copies ran while one was open for 3% of the time, Pallas kernels for 0%

profile of v3, /device:TPU:0, one launch (start us, length us, event | category | flops | bytes accessed | tf_op | source)
XLA Modules:
  0.0 204.6 jit_solution(320958194716182976)
XLA Ops:
  0.6 4.8 %reshape.68 = bf16[8,96,4,512]{3,2,1,0:T(4,128)(2,1)S(1)} reshape(bf16[1,768,2048]{2,1,0:T(8,128)(2,1)} %param.8) | data formatting | bytes 6291456 | tf_op jit(solution)/shard_map/reshape | solution.py:271
  5.4 2.5 %copy.19 = bf16[8,96,4,512]{3,1,2,0:T(8,128)(2,1)} copy(bf16[8,96,4,512]{3,2,1,0:T(4,128)(2,1)S(1)} %reshape.68) | data formatting | bytes 6291456 | tf_op jit(solution)/shard_map/reshape | solution.py:271
  7.9 0.0 copy-start.3
  7.9 0.0 copy-start.1
  7.9 7.3 %all-to-all-start = ((bf16[32,96,512]{2,1,0:T(8,128)(2,1)}), bf16[32,96,512]{2,1,0:T(8,128)(2,1)S(1)}, u32[]{:S(2)}, u32[]{:S(2)}) async-start(bf16[32,96,512]{2,1,0:T(8,128)(2,1)} %bitcast.2), calls=%async_computation | async-start | bytes 6291456 | tf_op jit(solution)/shard_map/all_to_all | solution.py:275
  15.2 0.0 copy-done.3
  15.2 0.1 copy.20
  15.3 0.1 reduce.1
  15.5 0.1 convert_reduce_fusion
  15.6 0.8 select_reduce_fusion
  16.3 0.5 convert_element_type.8
  16.8 0.7 copy.18
  17.6 0.1 reduce.last
  17.7 0.0 copy-start.2
  17.7 1.1 sub.3.first
  18.9 0.7 broadcast_in_dim.24
  19.6 0.0 copy-done.1
  19.6 0.8 pad_maximum_fusion.x_here
  20.4 64.9 %all-to-all-done.pieces = bf16[32,96,512]{2,1,0:T(8,128)(2,1)S(1)} async-done(((bf16[32,96,512]{2,1,0:T(8,128)(2,1)}), bf16[32,96,512]{2,1,0:T(8,128)(2,1)S(1)}, u32[]{:S(2)}, u32[]{:S(2)}) %all-to-all-start) | async-done | bytes 3145760 | tf_op jit(solution)/shard_map/all_to_all | solution.py:275
  85.4 0.0 copy-done.2
  85.4 0.0 copy-start
  85.4 1.7 copy-done
  87.0 14.7 %shard_map.111 = (bf16[16,96,512]{2,1,0:T(8,128)(2,1)}, f32[16,96,512]{2,1,0:T(8,128)}, f32[16,96,512]{2,1,0:T(8,128)}) custom-call(s32[16]{0:T(128)} %sub.3.first, s32[16]{0:T(128)} %copy-done.2, bf16[32,96,512]{2,1,0:T(8,128)(2,1)} %copy-done, bf16[16,96,512]{2,1,0:T(8,128)(2,1)} %w.1, f32[16,96,512]{2,1,0:T(8,128)} %m.1, f32[16,96,512]{2,1,0:T(8,128)} %v.1), custom_call_target="tpu_custom_call" | custom-call | tf_op jit(solution)/shard_map/pallas_call | solution.py:40
  101.8 100.5 %shard_map.112 = (bf16[256,2048]{1,0:T(8,128)(2,1)}, bf16[8,16,96,512]{3,2,1,0:T(8,128)(2,1)}) custom-call(bf16[256,896]{1,0:T(8,128)(2,1)} %pad_maximum_fusion.x_here, bf16[16,96,512]{2,1,0:T(8,128)(2,1)} %get-tuple-element.16.w_here), custom_call_target="tpu_custom_call" | custom-call | tf_op jit(solution)/shard_map/pallas_call | solution.py:229
  202.3 2.3 %copy.22 = bf16[256,2048]{1,0:T(8,128)(2,1)} copy(bf16[256,2048]{1,0:T(8,128)(2,1)} %get-tuple-element.19) | data formatting | bytes 2097152
  (2 shorter events, 0.1 us)
Async XLA Ops:
  7.9 7.3 %copy-start.3 = (s32[16]{0:T(128)S(1)}, s32[16]{0:T(128)}, u32[]{:S(2)}) copy-start(s32[16]{0:T(128)} %param.13) | copy-start | bytes 196
  7.9 11.7 %copy-start.1 = (bf16[256,768]{1,0:T(8,128)(2,1)S(1)}, bf16[256,768]{1,0:T(8,128)(2,1)}, u32[]{:S(2)}) copy-start(bf16[256,768]{1,0:T(8,128)(2,1)} %param.14) | copy-start | bytes 1179652
  7.9 77.5 %all-to-all-start = ((bf16[32,96,512]{2,1,0:T(8,128)(2,1)}), bf16[32,96,512]{2,1,0:T(8,128)(2,1)S(1)}, u32[]{:S(2)}, u32[]{:S(2)}) async-start(bf16[32,96,512]{2,1,0:T(8,128)(2,1)} %bitcast.2), calls=%async_computation | async-start | bytes 6291456 | tf_op jit(solution)/shard_map/all_to_all | solution.py:275
  17.7 67.7 %copy-start.2 = (s32[16]{0:T(128)}, s32[16]{0:T(128)S(1)}, u32[]{:S(2)}) copy-start(s32[16]{0:T(128)S(1)} %reduce.last) | copy-start | bytes 196
  85.4 1.7 copy-start
